TPU v7x, 1024 devices: a whole 4x8x16 slice. The times are simulated.
1024 devices in a mesh: fsdp: 32 (over z_hi, x, core), grp: 8 (over y), rep: 4 (over z_lo).
Axes of the slice: x: 4, y: 8, z: 16 (z_hi: 4, z_lo: 4; z = z_hi * 4 + z_lo), core: 2. Of those that a mesh axis runs over, the one named last changes fastest.
Arguments:
- iterate: bfloat16 [4096, 7168], P(('fsdp', 'grp', 'rep')), may hold values from -0.040283203 to 0.040283203
Outputs:
- update: bfloat16 [4096, 7168], P('fsdp', ('grp', 'rep'))
All inputs are finite; a program needn't handle non-finite values.
Results may differ from a plain program's by a relative error of at most 0.0059.
Values may be sent and summed in bfloat16 or wider, within the bound.
A program may use at most 32 MiB of HBM per device.

v0:
```python
import math

import jax
import jax.numpy as jnp
from jax import lax
from jax.sharding import PartitionSpec as P

COLS = 7168


coef_linear = 3.4445
coef_cubic = -4.775
coef_quintic = 2.0315


def body(iterate):
    holding = lax.all_to_all(iterate, ("grp", "rep"), split_axis=1, concat_axis=0, tiled=True)
    column_panel = lax.all_gather(holding, "fsdp", axis=0, tiled=True)
    partial_value = lax.dot_general(
        holding, column_panel, (((1,), (1,)), ((), ())), preferred_element_type=jnp.float32
    )
    gram_rows = lax.psum(partial_value, ("grp", "rep")).astype(jnp.bfloat16)
    first_image = jnp.dot(gram_rows, column_panel, preferred_element_type=jnp.float32).astype(
        jnp.bfloat16
    )
    second_image = jnp.dot(
        gram_rows,
        lax.all_gather(first_image, "fsdp", axis=0, tiled=True),
        preferred_element_type=jnp.float32,
    )
    factor = 0.2 * math.sqrt(COLS)
    combined = (
        coef_linear * holding.astype(jnp.float32)
        + coef_cubic * first_image.astype(jnp.float32)
        + coef_quintic * second_image
    )
    return (factor * combined).astype(jnp.bfloat16)


def solution(mesh):
    in_specs = (P(("fsdp", "grp", "rep"), None),)
    out_specs = P("fsdp", ("grp", "rep"))
    return jax.shard_map(body, mesh=mesh, in_specs=in_specs, out_specs=out_specs, check_vma=False)
```

profile of v0, /device:TPU:1, one launch (start us, length us, event | category | flops | bytes accessed | tf_op | source)
XLA Modules:
  0.0 408.1 jit_solution(4531051256717405805)
XLA Ops:
  6.5 0.0 all-gather.3.cloned.1.call-start
  6.5 0.9 all_to_all.14
  7.5 0.1 copy.3
  7.5 22.6 %all_to_all.19 = bf16[4,32,224]{2,0,1:T(4,128)(2,1)S(1)} all-to-all(bf16[4,32,224]{2,0,1:T(4,128)(2,1)S(1)} %copy.3), channel_id=1, replica_groups=mesh['fsdp'=32,'grp'=8,'rep'=4] {'grp','rep'}, dimensions={1} | all-to-all | bytes 114688 | tf_op jit(solution)/shard_map/all_to_all | solution.py:17
  30.2 0.7 all_to_all.17
  30.8 0.0 all-gather.3.cloned.1.call-update
  30.9 0.0 all-gather.5.cloned.1.call-start
  30.9 87.7 %all-gather.3.cloned.1.call-done = bf16[4096,224]{1,0:T(8,128)(2,1)} async-done(((bf16[128,224]{1,0:T(8,128)(2,1)}), bf16[4096,224]{1,0:T(8,128)(2,1)}) %all-gather.3.cloned.1.call-update) | async-done | bytes 1835024 | tf_op jit(solution)/shard_map/all_gather | solution.py:18
  118.6 3.7 fusion.5
  122.3 0.0 copy-start
  122.3 167.6 %all-reduce.1 = bf16[128,4096]{1,0:T(8,128)(2,1)S(1)} all-reduce(f32[128,4096]{1,0:T(8,128)} %fusion.5), channel_id=1, replica_groups=mesh['fsdp'=32,'grp'=8,'rep'=4] {'grp','rep'}, use_global_device_ids=true, to_apply=%region_0.0 | all-reduce | flops 524288 | bytes 3145728 | tf_op jit(solution)/shard_map/psum | solution.py:22
  289.9 0.0 copy-done
  289.9 0.0 copy-start.1
  289.9 1.5 convolution_convert_fusion
  291.5 0.0 all-gather.5.cloned.1.call-update
  291.5 0.0 copy-done.1
  291.5 0.1 copy.4
  291.6 106.9 %all-gather.5.cloned.1.call-done = bf16[4096,224]{0,1:T(8,128)(2,1)} async-done(((bf16[128,224]{0,1:T(8,128)(2,1)}), bf16[4096,224]{0,1:T(8,128)(2,1)}) %all-gather.5.cloned.1.call-update) | async-done | bytes 1835024 | tf_op jit(solution)/shard_map/all_gather | solution.py:28
  398.5 2.8 fusion.2
Async XLA Ops:
  6.5 112.1 %all-gather.3.cloned.1.call-start = ((), (), s32[]{:S(2)}) async-start(), calls=%async_computation.1 | async-start | bytes 2162688 | tf_op jit(solution)/shard_map/all_gather | solution.py:18
  30.9 367.6 %all-gather.5.cloned.1.call-start = ((), (), s32[]{:S(2)}) async-start(), calls=%async_computation.2 | async-start | bytes 1892352 | tf_op jit(solution)/shard_map/all_gather | solution.py:28
  122.3 167.6 %copy-start = (bf16[4096,224]{1,0:T(8,128)(2,1)S(1)}, bf16[4096,224]{1,0:T(8,128)(2,1)}, u32[]{:S(2)}) copy-start(bf16[4096,224]{1,0:T(8,128)(2,1)} %all-gather.3.cloned.1.call-done) | copy-start | bytes 5505028
  289.9 1.6 copy-start.1
Sparse Core Ops, SparseCore 0:
  31.0 87.5 all-gather.2
  291.6 106.8 all-gather.4
where the time goes:
time: 408 us
  waiting for transfers between devices  195 us (48%)
  blocking collectives  190 us (47%)
  between operations  13.4 us (3%)
  matrix products  8.03 us (2%)
    psum x1, blocking collectives, body(): gram_rows = lax.psum(partial_value, ('grp', 'rep')).astype(jnp.bfloat16)  168 us
    all_gather x1, waiting for transfers between devices, body(): lax.all_gather(first_image, 'fsdp', axis=0, tiled=True)  107 us
    all_gather x1, waiting for transfers between devices, body(): column_panel = lax.all_gather(holding, 'fsdp', axis=0, tiled=True)  87.7 us
    all_to_all x1, blocking collectives, body(): lax.all_to_all(iterate, ('grp', 'rep'), split_axis=1, concat_axis=0, tile...  22.6 us
  transfers between devices with their start and end apart: 2, of which 2 were waited for; matrix products, arithmetic and copies ran while one was open for 0% of the time, Pallas kernels for 0%

commit v1 on v0

v1 whole, which is shorter than its diff:
```python
import functools
import math

import jax
import jax.numpy as jnp
from jax import lax
from jax.experimental import pallas as pl
from jax.experimental.pallas import tpu as pltpu
from jax.sharding import PartitionSpec as P

COLS = 7168

coef_linear = 3.4445
coef_cubic = -4.775
coef_quintic = 2.0315

MESH = pl.DeviceIdType.MESH
NZ, NX, NC = 4, 4, 2
NY, NL = 8, 4
OWN = 4
PIECE = NY * OWN
ROWS = NL * PIECE
WIDTH = COLS // NY
NARROW = WIDTH // NL
GROUP = NX * NC * PIECE
STRIP = ROWS // NY
Z_ORDER = (1, 3, 2)


def kernel(
    w_ref, o_ref, raw, rows32, left, panel, gram_part, gram_in, gram, first_part, first_in, first, out_part, out_in, acc,
    s_a, r_a, s_l, r_l, s_z, r_z, s_x, r_x, s_c, r_c, s_g, r_g, s_d, r_d, s_f, r_f, s_o, r_o,
):
    at = lax.axis_index("fsdp")
    y = lax.axis_index("grp")
    zl = lax.axis_index("rep")
    zh, x, c = at // (NX * NC), (at // NC) % NX, at % NC

    def far(dz=0, dx=0, dc=0, dy=0, dl=0):
        f = (((zh + dz) % NZ) * NX + (x + dx) % NX) * NC + (c + dc) % NC
        return (f, (y + dy) % NY, (zl + dl) % NL)

    partners = [far(dy=k) for k in range(1, NY)] + [far(dl=k) for k in range(1, NL)]
    partners += [far(dz=k) for k in range(1, NZ)] + [far(dx=k) for k in range(1, NX)] + [far(dc=1)]
    barrier = pltpu.get_barrier_semaphore()
    for partner in partners:
        pl.semaphore_signal(barrier, inc=1, device_id=partner, device_id_type=MESH)
    pl.semaphore_wait(barrier, len(partners))

    sent = []

    def send(src, dst, s, r, to):
        copy = pltpu.make_async_remote_copy(
            src_ref=src, dst_ref=dst, send_sem=s, recv_sem=r, device_id=to, device_id_type=MESH
        )
        copy.start()
        sent.append(copy)

    def arrived(dst, s, r):
        pltpu.make_async_remote_copy(
            src_ref=dst, dst_ref=dst, send_sem=s, recv_sem=r, device_id=far(dc=1), device_id_type=MESH
        ).wait_recv()

    for k in range(1, NY):
        to = lax.rem(y + k, NY)
        cols = pl.ds(pl.multiple_of(to * WIDTH, 128), WIDTH)
        send(w_ref.at[:, cols], raw.at[y], s_a.at[k], r_a.at[k], far(dy=k))
    raw[y] = w_ref[:, pl.ds(pl.multiple_of(y * WIDTH, 128), WIDTH)]
    for k in range(1, NY):
        arrived(raw.at[lax.rem(y + NY - k, NY)], s_a.at[k], r_a.at[k])
    for k in range(NY):
        rows32[OWN * k : OWN * (k + 1), :] = raw[k].astype(jnp.float32)
    own = rows32[...].astype(jnp.bfloat16)
    panel[0, 0, 0] = own
    left[zl] = own

    def spread_z(buf, p):
        for k in Z_ORDER:
            send(buf.at[0, 0, 0], buf.at[NZ - k, 0, 0], s_z.at[p, NZ - k], r_z.at[p, NZ - k], far(dz=k))

    def spread_x(buf, p, g):
        if g > 0:
            arrived(buf.at[g, 0, 0], s_z.at[p, g], r_z.at[p, g])
        for k in (1, 3, 2):
            send(buf.at[g, 0, 0], buf.at[g, NX - k, 0], s_x.at[p, g, NX - k], r_x.at[p, g, NX - k], far(dx=k))
        send(buf.at[g, 0, 0], buf.at[g, 0, 1], s_c.at[p, g, 0], r_c.at[p, g, 0], far(dc=1))

    def spread_c(buf, p, g):
        for k in (1, 3, 2):
            arrived(buf.at[g, k, 0], s_x.at[p, g, k], r_x.at[p, g, k])
            send(buf.at[g, k, 0], buf.at[g, k, 1], s_c.at[p, g, k], r_c.at[p, g, k], far(dc=1))

    def whole(buf, p, g):
        for k in range(NX):
            arrived(buf.at[g, k, 1], s_c.at[p, g, k], r_c.at[p, g, k])
        return buf[g].reshape(GROUP, WIDTH)

    def gram_send(g):
        part = lax.dot_general(
            left[...].reshape(ROWS, WIDTH), whole(panel, 0, g), (((1,), (1,)), ((), ())),
            preferred_element_type=jnp.float32,
        )
        gram_part[g] = part.astype(jnp.bfloat16).reshape(NY, STRIP, GROUP)
        for k in range(1, NY):
            to = lax.rem(y + k, NY)
            send(gram_part.at[g, to], gram_in.at[g, k], s_g.at[g, k], r_g.at[g, k], far(dy=k))

    def gram_sum(g):
        total = gram_part[g, y].astype(jnp.float32)
        for k in range(1, NY):
            arrived(gram_in.at[g, k], s_g.at[g, k], r_g.at[g, k])
            total = total + gram_in[g, k].astype(jnp.float32)
        gram[g, y] = total.astype(jnp.bfloat16)
        for k in range(1, NY):
            send(gram.at[g, y], gram.at[g, y], s_d.at[g, k], r_d.at[g, k], far(dy=k))

    def times(g, right, start):
        add = jnp.dot(gram[g].reshape(ROWS, GROUP), right, preferred_element_type=jnp.float32)
        if start:
            acc[...] = add
        else:
            acc[...] += add

    spread_z(panel, 0)
    for k in range(1, NL):
        send(left.at[zl], left.at[zl], s_l.at[k], r_l.at[k], far(dl=k))
    spread_x(panel, 0, 0)
    spread_x(panel, 0, 1)
    spread_x(panel, 0, 3)
    spread_c(panel, 0, 0)
    for k in range(1, NL):
        arrived(left.at[lax.rem(zl + NL - k, NL)], s_l.at[k], r_l.at[k])
    gram_send(0)
    spread_c(panel, 0, 1)
    spread_x(panel, 0, 2)
    gram_send(1)
    spread_c(panel, 0, 3)
    gram_send(3)
    gram_sum(0)
    spread_c(panel, 0, 2)
    gram_send(2)
    gram_sum(1)
    gram_sum(3)
    gram_sum(2)

    for n, g in enumerate((0, 1, 3, 2)):
        for k in range(1, NY):
            arrived(gram.at[g, lax.rem(y + NY - k, NY)], s_d.at[g, k], r_d.at[g, k])
        times(g, panel[g].reshape(GROUP, WIDTH), n == 0)
    first_part[...] = acc[...].astype(jnp.bfloat16).reshape(NL, PIECE, WIDTH)
    for k in range(1, NL):
        to = lax.rem(zl + k, NL)
        send(first_part.at[to], first_in.at[k], s_f.at[k], r_f.at[k], far(dl=k))
    total = first_part[zl].astype(jnp.float32)
    for k in range(1, NL):
        arrived(first_in.at[k], s_f.at[k], r_f.at[k])
        total = total + first_in[k].astype(jnp.float32)
    first[0, 0, 0] = total.astype(jnp.bfloat16)

    spread_z(first, 1)
    spread_x(first, 1, 0)
    spread_x(first, 1, 1)
    spread_x(first, 1, 3)
    spread_c(first, 1, 0)
    times(0, whole(first, 1, 0), True)
    spread_c(first, 1, 1)
    times(1, whole(first, 1, 1), False)
    spread_x(first, 1, 2)
    spread_c(first, 1, 3)
    times(3, whole(first, 1, 3), False)
    spread_c(first, 1, 2)
    times(2, whole(first, 1, 2), False)

    factor = 0.2 * math.sqrt(COLS)
    acc[...] = (factor * coef_quintic) * acc[...]
    mine = pl.ds(pl.multiple_of(zl * PIECE, PIECE), PIECE)
    acc[mine, :] += factor * (
        coef_linear * panel[0, 0, 0].astype(jnp.float32) + coef_cubic * first[0, 0, 0].astype(jnp.float32)
    )
    for k in range(NL):
        out_part[k] = acc[:, NARROW * k : NARROW * (k + 1)].astype(jnp.bfloat16)
    for k in range(1, NL):
        to = lax.rem(zl + k, NL)
        send(out_part.at[to], out_in.at[k], s_o.at[k], r_o.at[k], far(dl=k))
    total = out_part[zl].astype(jnp.float32)
    for k in range(1, NL):
        arrived(out_in.at[k], s_o.at[k], r_o.at[k])
        total = total + out_in[k].astype(jnp.float32)
    to_row = lax.broadcasted_iota(jnp.int32, (ROWS, ROWS), 0)
    from_row = lax.broadcasted_iota(jnp.int32, (ROWS, ROWS), 1)
    source = ((to_row // OWN) % NL) * PIECE + (to_row // (OWN * NL)) * OWN + to_row % OWN
    order = (source == from_row).astype(jnp.float32).astype(jnp.bfloat16)
    o_ref[...] = jnp.dot(order, total.astype(jnp.bfloat16), preferred_element_type=jnp.float32).astype(jnp.bfloat16)

    for copy in sent:
        copy.wait_send()


def body(iterate):
    bf, f32, dma = jnp.bfloat16, jnp.float32, pltpu.SemaphoreType.DMA
    vm = pltpu.VMEM
    counts = [(NY,), (NL,), (2, NZ), (2, NZ, NX), (2, NZ, NX), (NZ, NY), (NZ, NY), (NL,), (NL,)]
    sems = [dma(n) for n in counts for _ in range(2)]
    return pl.pallas_call(
        kernel,
        out_shape=jax.ShapeDtypeStruct((ROWS, NARROW), bf),
        in_specs=[pl.BlockSpec(memory_space=pltpu.VMEM)],
        out_specs=pl.BlockSpec(memory_space=pltpu.VMEM),
        scratch_shapes=[
            vm((NY, OWN, WIDTH), bf),
            vm((PIECE, WIDTH), f32),
            vm((NL, PIECE, WIDTH), bf),
            vm((NZ, NX, NC, PIECE, WIDTH), bf),
            vm((NZ, NY, STRIP, GROUP), bf),
            vm((NZ, NY, STRIP, GROUP), bf),
            vm((NZ, NY, STRIP, GROUP), bf),
            vm((NL, PIECE, WIDTH), bf),
            vm((NL, PIECE, WIDTH), bf),
            vm((NZ, NX, NC, PIECE, WIDTH), bf),
            vm((NL, ROWS, NARROW), bf),
            vm((NL, ROWS, NARROW), bf),
            vm((ROWS, WIDTH), f32),
        ] + sems,
        compiler_params=pltpu.CompilerParams(collective_id=0, has_side_effects=True, vmem_limit_bytes=32 << 20),
        cost_estimate=pl.CostEstimate(flops=6 * ROWS * GROUP * NZ * WIDTH, bytes_accessed=4 * ROWS * NARROW, transcendentals=0),
    )(iterate)


def solution(mesh):
    in_specs = (P(("fsdp", "grp", "rep"), None),)
    out_specs = P("fsdp", ("grp", "rep"))
    return jax.shard_map(body, mesh=mesh, in_specs=in_specs, out_specs=out_specs, check_vma=False)
```

time: 408 us -> 102 us (0.25)
  waiting for transfers between devices: 195 us -> 0 us
  blocking collectives: 190 us -> 0 us
  Pallas kernels: 0 us -> 99.8 us
  between operations: 13.4 us -> 0.01 us
  matrix products: 8.03 us -> 0 us
    all_gather x2 -> x0, waiting for transfers between devices: 195 us -> none  [the longest x1 107 us: body(): lax.all_gather(first_image, 'fsdp', axis=0, tiled=True)]
    psum x1 -> x0, blocking collectives: 168 us -> none  [body(): gram_rows = lax.psum(partial_value, ('grp', 'rep')).astype(jnp.bfloat16)]
    pallas_call x0 -> x1, Pallas kernels: none -> 99.8 us  [body(): pl.pallas_call(kernel, out_shape=jax.ShapeDtypeStruct((ROWS, NARROW), bf)...]
    all_to_all x1 -> x0, blocking collectives: 22.6 us -> none  [body(): lax.all_to_all(iterate, ('grp', 'rep'), split_axis=1, concat_axis=0, tile...]
    dot_general x3 -> x0, matrix products: 8.03 us -> none  [the longest x1 3.74 us: body(): lax.dot_general(holding, column_panel, (((1,), (1,)), ((), ())), preferre...]
  transfers between devices with their start and end apart: 2 -> 0, of which waited for: 2 -> 0; matrix products, arithmetic and copies ran while one was open for 0% -> 0% of each run, Pallas kernels for 0% -> 0%
where the time goes in v1:
time: 102 us; the launch traced here: 101 us
  Pallas kernels  99.8 us (98%)
  local copies, waits for them, and re-layouts  1.54 us (2%)
    pallas_call x1, Pallas kernels, body(): pl.pallas_call(kernel, out_shape=jax.ShapeDtypeStruct((ROWS, NARROW), bf)...  99.8 us

profile of v1, /device:TPU:1, one launch (start us, length us, event | category | flops | bytes accessed | tf_op | source)
XLA Modules:
  0.0 101.3 jit_solution(6356853590155751589)
XLA Ops:
  0.0 0.0 copy-start
  0.0 0.8 copy-done
  0.8 99.8 %shard_map.17 = bf16[128,224]{1,0:T(8,128)(2,1)S(1)} custom-call(bf16[4,7168]{1,0:T(4,128)(2,1)S(1)} %copy-done), custom_call_target="tpu_custom_call" | custom-call | flops 704643072 | bytes 114688 | tf_op jit(solution)/shard_map/pallas_call | solution.py:204
  100.6 0.7 copy.2
Async XLA Ops:
  0.0 0.8 copy-start

commit v2 on v0

v2 whole, which is shorter than its diff:
```python
import math

import jax
import jax.numpy as jnp
from jax import lax
from jax.experimental import pallas as pl
from jax.experimental.pallas import tpu as pltpu
from jax.sharding import PartitionSpec as P

COLS = 7168

coef_linear = 3.4445
coef_cubic = -4.775
coef_quintic = 2.0315

MESH = pl.DeviceIdType.MESH
NZ, NX, NC = 4, 4, 2
NY, NL = 8, 4
OWN = 4
PIECE = NY * OWN
HALF = NL * PIECE
ROWS = NC * HALF
WIDTH = COLS // NY
NARROW = WIDTH // NL
GROUP = NX * PIECE
STRIP = ROWS // NY
AROUND = (1, 3, 2)
CHUNKS = ((0, 512), (512, 384))
LAST = len(CHUNKS) - 1
FIRST_PLAN = (
    ("x", 0, 0), ("x", 1, 0), ("x", 0, 3), ("x", 1, 1), ("x", 0, 1), ("x", 1, 3), ("u", 0, 0),
    ("u", 1, 0), ("x", 0, 2), ("x", 1, 2), ("u", 0, 1), ("u", 1, 1), ("u", 0, 3), ("u", 1, 3),
    ("s", 0, 0), ("s", 0, 1), ("u", 0, 2), ("u", 1, 2), ("s", 0, 3), ("s", 0, 2),
)
SECOND_PLAN = (
    ("x", 0, 0), ("x", 1, 0), ("x", 0, 3), ("x", 0, 1), ("u", 0, 0), ("x", 1, 1), ("x", 1, 3),
    ("u", 0, 1), ("u", 0, 3), ("x", 0, 2), ("u", 1, 0), ("x", 1, 2), ("u", 1, 1), ("u", 1, 3),
    ("u", 0, 2), ("o", 0, 0), ("u", 1, 2), ("o", 1, 0),
)
ORDER = (0, 1, 3, 2)
RELAY = ((0, 3), (1, 1))


def kernel(
    w_ref, o_ref, raw, rows32, left, panel, gram32, gram_part, gram_in, gram, pair_out, pair_in, first_part, first_in,
    first, out_all, out_part, out_in, acc, gram_acc,
    s_a, r_a, s_l, r_l, s_m, r_m, s_z, r_z, s_x, r_x, s_g, r_g, s_d, r_d, s_p, r_p, s_f, r_f, s_o, r_o,
):
    at = lax.axis_index("fsdp")
    y = lax.axis_index("grp")
    zl = lax.axis_index("rep")
    zh, x, c = lax.div(at, NX * NC), lax.rem(lax.div(at, NC), NX), lax.rem(at, NC)

    def step(start, by, size):
        return lax.rem(start + by, size)

    line_y = [(at, step(y, k, NY), zl) for k in range(NY)]
    line_l = [(at, y, step(zl, k, NL)) for k in range(NL)]
    line_x = [(zh * (NX * NC) + step(x, k, NX) * NC + c, y, zl) for k in range(NX)]
    line_z = [(step(zh, k, NZ) * (NX * NC) + x * NC + c, y, zl) for k in range(NZ)]
    other = (zh * (NX * NC) + x * NC + (1 - c), y, zl)

    partners = line_y[1:] + line_l[1:] + line_x[1:] + [line_z[1], line_z[3], other]
    barrier = pltpu.get_barrier_semaphore()
    for partner in partners:
        pl.semaphore_signal(barrier, inc=1, device_id=partner, device_id_type=MESH)
    pl.semaphore_wait(barrier, len(partners))

    sent = []

    def send(src, dst, s, r, to):
        copy = pltpu.make_async_remote_copy(
            src_ref=src, dst_ref=dst, send_sem=s, recv_sem=r, device_id=to, device_id_type=MESH
        )
        copy.start()
        sent.append(copy)

    def arrived(dst, s, r):
        pltpu.make_async_remote_copy(
            src_ref=dst, dst_ref=dst, send_sem=s, recv_sem=r, device_id=other, device_id_type=MESH
        ).wait_recv()

    def to_line(to):
        return w_ref.at[:, pl.ds(pl.multiple_of(to * WIDTH, 128), WIDTH)]

    for k in range(1, NY):
        send(to_line(step(y, k, NY)), raw.at[y], s_a.at[k], r_a.at[k], line_y[k])
    keep = pltpu.make_async_copy(to_line(y), raw.at[y], s_a.at[0])
    keep.start()
    keep.wait()
    for k in range(1, NY):
        arrived(raw.at[step(y, NY - k, NY)], s_a.at[k], r_a.at[k])
    for k in range(NY):
        rows32[OWN * k : OWN * (k + 1), :] = raw[k].astype(jnp.float32)
    own = rows32[...].astype(jnp.bfloat16)
    panel[0, 0] = own
    left[c, zl] = own

    def part(buf, g, k, n):
        return buf.at[g, k, :, pl.ds(CHUNKS[n][0], CHUNKS[n][1])]

    def z_out(buf, p, n):
        for k in (1, 3):
            send(part(buf, 0, 0, n), part(buf, NZ - k, 0, n), s_z.at[p, n, NZ - k], r_z.at[p, n, NZ - k], line_z[k])

    def spread(buf, p, plan, use, rest):
        for what, n, g in plan:
            if what == "x":
                if g > 0:
                    arrived(part(buf, g, 0, n), s_z.at[p, n, g], r_z.at[p, n, g])
                if (n, g) in RELAY:
                    send(part(buf, g, 0, n), part(buf, 2, 0, n), s_z.at[p, n, 2], r_z.at[p, n, 2], line_z[NZ - g])
                for k in AROUND:
                    to = NX - k
                    send(part(buf, g, 0, n), part(buf, g, to, n), s_x.at[p, n, g, to], r_x.at[p, n, g, to], line_x[k])
            elif what == "u":
                for k in AROUND:
                    arrived(part(buf, g, k, n), s_x.at[p, n, g, k], r_x.at[p, n, g, k])
                use(n, g)
            else:
                rest(n, g)

    def columns(buf, g, n):
        return buf[g, :, :, CHUNKS[n][0] : CHUNKS[n][0] + CHUNKS[n][1]].reshape(GROUP, CHUNKS[n][1])

    def gram_step(n, g):
        if (n, g) == (0, 0):
            for k in range(1, NL):
                who = step(zl, NL - k, NL)
                arrived(left.at[c, who], s_l.at[k], r_l.at[k])
                send(left.at[c, who], left.at[c, who], s_m.at[k], r_m.at[k], other)
            for k in range(NL):
                arrived(left.at[1 - c, step(zl, NL - k, NL)], s_m.at[k], r_m.at[k])
        lo, size = CHUNKS[n]
        add = lax.dot_general(
            left[:, :, :, lo : lo + size].reshape(ROWS, size), columns(panel, g, n), (((1,), (1,)), ((), ())),
            preferred_element_type=jnp.float32,
        )
        if n < LAST:
            gram_acc[...] = add if n == 0 else gram_acc[...] + add
            return
        total = (gram_acc[...] + add).reshape(NY, STRIP, GROUP)
        gram32[g] = total
        gram_part[g] = total.astype(jnp.bfloat16)
        for k in range(1, NY):
            send(gram_part.at[g, step(y, k, NY)], gram_in.at[g, k], s_g.at[g, k], r_g.at[g, k], line_y[k])

    def gram_sum(n, g):
        total = gram32[g, y]
        for k in range(1, NY):
            arrived(gram_in.at[g, k], s_g.at[g, k], r_g.at[g, k])
            total = total + gram_in[g, k].astype(jnp.float32)
        gram[g, y] = total.astype(jnp.bfloat16)
        for k in range(1, NY):
            send(gram.at[g, y], gram.at[g, y], s_d.at[g, k], r_d.at[g, k], line_y[k])

    def times(buf, n, g):
        add = jnp.dot(gram[g].reshape(ROWS, GROUP), columns(buf, g, n), preferred_element_type=jnp.float32)
        lo, size = CHUNKS[n]
        if g == ORDER[0]:
            acc[:, lo : lo + size] = add
        else:
            acc[:, lo : lo + size] += add

    half = pl.ds(pl.multiple_of(c * HALF, HALF), HALF)
    other_half = pl.ds(pl.multiple_of((1 - c) * HALF, HALF), HALF)
    mine = pl.ds(pl.multiple_of(c * HALF + zl * PIECE, PIECE), PIECE)

    def pair_send(p, n):
        lo, size = CHUNKS[n]
        cut = pl.ds(lo, size)
        pair_out[p, :, lo : lo + size] = acc[other_half, lo : lo + size].astype(jnp.bfloat16)
        send(pair_out.at[p, :, cut], pair_in.at[p, :, cut], s_p.at[p, n], r_p.at[p, n], other)

    def pair_add(p, n):
        lo, size = CHUNKS[n]
        arrived(pair_in.at[p, :, pl.ds(lo, size)], s_p.at[p, n], r_p.at[p, n])
        acc[half, lo : lo + size] += pair_in[p, :, lo : lo + size].astype(jnp.float32)

    for n in range(len(CHUNKS)):
        z_out(panel, 0, n)
    send(left.at[c, zl], left.at[c, zl], s_m.at[0], r_m.at[0], other)
    for k in range(1, NL):
        send(left.at[c, zl], left.at[c, zl], s_l.at[k], r_l.at[k], line_l[k])
    spread(panel, 0, FIRST_PLAN, gram_step, gram_sum)

    for g in ORDER:
        for k in range(1, NY):
            arrived(gram.at[g, step(y, NY - k, NY)], s_d.at[g, k], r_d.at[g, k])
        for n in range(len(CHUNKS)):
            times(panel, n, g)
            if g == ORDER[-1]:
                pair_send(0, n)
    for n, (lo, size) in enumerate(CHUNKS):
        pair_add(0, n)
        cut = pl.ds(lo, size)
        first_part[:, :, lo : lo + size] = acc[half, lo : lo + size].astype(jnp.bfloat16).reshape(NL, PIECE, size)
        for k in range(1, NL):
            to = first_part.at[step(zl, k, NL), :, cut]
            send(to, first_in.at[k, :, cut], s_f.at[n, k], r_f.at[n, k], line_l[k])
    for n, (lo, size) in enumerate(CHUNKS):
        total = acc[mine, lo : lo + size]
        for k in range(1, NL):
            arrived(first_in.at[k, :, pl.ds(lo, size)], s_f.at[n, k], r_f.at[n, k])
            total = total + first_in[k, :, lo : lo + size].astype(jnp.float32)
        first[0, 0, :, lo : lo + size] = total.astype(jnp.bfloat16)
        z_out(first, 1, n)

    factor = 0.2 * math.sqrt(COLS)

    def second_step(n, g):
        times(first, n, g)
        if g == ORDER[-1]:
            pair_send(1, n)

    def out_step(n, g):
        pair_add(1, n)
        lo, size = CHUNKS[n]
        acc[mine, lo : lo + size] += (coef_linear / coef_quintic) * panel[0, 0, :, lo : lo + size].astype(jnp.float32) + (
            coef_cubic / coef_quintic
        ) * first[0, 0, :, lo : lo + size].astype(jnp.float32)
        out_all[:, lo : lo + size] = ((factor * coef_quintic) * acc[half, lo : lo + size]).astype(jnp.bfloat16)
        for q in range(NL):
            if lo < NARROW * (q + 1) <= lo + size:
                out_part[q] = out_all[:, NARROW * q : NARROW * (q + 1)]

                @pl.when(zl != q)
                def _():
                    pltpu.make_async_remote_copy(
                        src_ref=out_part.at[q], dst_ref=out_in.at[zl], send_sem=s_o.at[q], recv_sem=r_o.at[zl],
                        device_id=(at, y, q), device_id_type=MESH,
                    ).start()

    spread(first, 1, SECOND_PLAN, second_step, out_step)
    total = out_part[zl].astype(jnp.float32)
    for k in range(1, NL):
        who = step(zl, NL - k, NL)
        arrived(out_in.at[who], s_o.at[who], r_o.at[who])
        total = total + out_in[who].astype(jnp.float32)
    to_row = lax.broadcasted_iota(jnp.int32, (HALF, HALF), 0)
    from_row = lax.broadcasted_iota(jnp.int32, (HALF, HALF), 1)
    source = ((to_row // OWN) % NL) * PIECE + (to_row // (OWN * NL)) * OWN + to_row % OWN
    order = (source == from_row).astype(jnp.float32).astype(jnp.bfloat16)
    o_ref[...] = jnp.dot(order, total.astype(jnp.bfloat16), preferred_element_type=jnp.float32).astype(jnp.bfloat16)

    for k in range(1, NL):
        who = step(zl, k, NL)
        pltpu.make_async_remote_copy(
            src_ref=out_part.at[who], dst_ref=out_in.at[zl], send_sem=s_o.at[who], recv_sem=r_o.at[zl],
            device_id=(at, y, who), device_id_type=MESH,
        ).wait_send()
    for copy in sent:
        copy.wait_send()


def body(iterate):
    bf, f32, dma = jnp.bfloat16, jnp.float32, pltpu.SemaphoreType.DMA
    vm = pltpu.VMEM
    n = len(CHUNKS)
    counts = [(NY,), (NL,), (NL,), (2, n, NZ), (2, n, NZ, NX), (NZ, NY), (NZ, NY), (2, n), (n, NL), (NL,)]
    sems = [dma(count) for count in counts for _ in range(2)]
    return pl.pallas_call(
        kernel,
        out_shape=jax.ShapeDtypeStruct((HALF, NARROW), bf),
        in_specs=[pl.BlockSpec(memory_space=pl.ANY)],
        out_specs=pl.BlockSpec(memory_space=pltpu.VMEM),
        scratch_shapes=[
            vm((NY, OWN, WIDTH), bf),
            vm((PIECE, WIDTH), f32),
            vm((NC, NL, PIECE, WIDTH), bf),
            vm((NZ, NX, PIECE, WIDTH), bf),
            vm((NZ, NY, STRIP, GROUP), f32),
            vm((NZ, NY, STRIP, GROUP), bf),
            vm((NZ, NY, STRIP, GROUP), bf),
            vm((NZ, NY, STRIP, GROUP), bf),
            vm((2, HALF, WIDTH), bf),
            vm((2, HALF, WIDTH), bf),
            vm((NL, PIECE, WIDTH), bf),
            vm((NL, PIECE, WIDTH), bf),
            vm((NZ, NX, PIECE, WIDTH), bf),
            vm((HALF, WIDTH), bf),
            vm((NL, HALF, NARROW), bf),
            vm((NL, HALF, NARROW), bf),
            vm((ROWS, WIDTH), f32),
            vm((ROWS, GROUP), f32),
        ] + sems,
        compiler_params=pltpu.CompilerParams(collective_id=0, has_side_effects=True, vmem_limit_bytes=32 << 20),
        cost_estimate=pl.CostEstimate(flops=6 * ROWS * GROUP * NZ * WIDTH, bytes_accessed=4 * HALF * NARROW, transcendentals=0),
    )(iterate)


def solution(mesh):
    in_specs = (P(("fsdp", "grp", "rep"), None),)
    out_specs = P("fsdp", ("grp", "rep"))
    return jax.shard_map(body, mesh=mesh, in_specs=in_specs, out_specs=out_specs, check_vma=False)
```

time: 408 us -> 94.1 us (0.23)
  waiting for transfers between devices: 195 us -> 0 us
  blocking collectives: 190 us -> 0 us
  Pallas kernels: 0 us -> 92.4 us
  between operations: 13.4 us -> 0.01 us
  matrix products: 8.03 us -> 0 us
    all_gather x2 -> x0, waiting for transfers between devices: 195 us -> none  [the longest x1 107 us: body(): lax.all_gather(first_image, 'fsdp', axis=0, tiled=True)]
    psum x1 -> x0, blocking collectives: 168 us -> none  [body(): gram_rows = lax.psum(partial_value, ('grp', 'rep')).astype(jnp.bfloat16)]
    pallas_call x0 -> x1, Pallas kernels: none -> 92.4 us  [body(): pl.pallas_call(kernel, out_shape=jax.ShapeDtypeStruct((HALF, NARROW), bf)...]
    all_to_all x1 -> x0, blocking collectives: 22.6 us -> none  [body(): lax.all_to_all(iterate, ('grp', 'rep'), split_axis=1, concat_axis=0, tile...]
    dot_general x3 -> x0, matrix products: 8.03 us -> none  [the longest x1 3.74 us: body(): lax.dot_general(holding, column_panel, (((1,), (1,)), ((), ())), preferre...]
  transfers between devices with their start and end apart: 2 -> 0, of which waited for: 2 -> 0; matrix products, arithmetic and copies ran while one was open for 0% -> 0% of each run, Pallas kernels for 0% -> 0%
where the time goes in v2:
time: 94.1 us; the launch traced here: 93.9 us
  Pallas kernels  92.4 us (98%)
  local copies, waits for them, and re-layouts  1.54 us (2%)
    pallas_call x1, Pallas kernels, body(): pl.pallas_call(kernel, out_shape=jax.ShapeDtypeStruct((HALF, NARROW), bf)...  92.4 us

profile of v2, /device:TPU:1, one launch (start us, length us, event | category | flops | bytes accessed | tf_op | source)
XLA Modules:
  0.0 93.9 jit_solution(1256132008101995960)
XLA Ops:
  0.0 0.0 copy-start
  0.0 0.8 copy-done
  0.8 92.4 %shard_map.17 = bf16[128,224]{1,0:T(8,128)(2,1)S(1)} custom-call(bf16[4,7168]{1,0:T(4,128)(2,1)S(1)} %copy-done), custom_call_target="tpu_custom_call" | custom-call | flops 704643072 | bytes 114688 | tf_op jit(solution)/shard_map/pallas_call | solution.py:262
  93.2 0.7 copy.2
Async XLA Ops:
  0.0 0.8 copy-start

commit v3 on v2

--- a/solution.py
+++ b/solution.py
@@ -24,7 +24,7 @@
 NARROW = WIDTH // NL
 GROUP = NX * PIECE
 STRIP = ROWS // NY
-AROUND = (1, 3, 2)
+AROUND = (2, 1, 3)
 CHUNKS = ((0, 512), (512, 384))
 LAST = len(CHUNKS) - 1
 FIRST_PLAN = (
@@ -83,7 +83,7 @@
     def to_line(to):
         return w_ref.at[:, pl.ds(pl.multiple_of(to * WIDTH, 128), WIDTH)]
 
-    for k in range(1, NY):
+    for k in (4, 3, 5, 2, 6, 1, 7):
         send(to_line(step(y, k, NY)), raw.at[y], s_a.at[k], r_a.at[k], line_y[k])
     keep = pltpu.make_async_copy(to_line(y), raw.at[y], s_a.at[0])
     keep.start()
@@ -100,7 +100,7 @@
         return buf.at[g, k, :, pl.ds(CHUNKS[n][0], CHUNKS[n][1])]
 
     def z_out(buf, p, n):
-        for k in (1, 3):
+        for k in ((1, 3), (3, 1))[n]:
             send(part(buf, 0, 0, n), part(buf, NZ - k, 0, n), s_z.at[p, n, NZ - k], r_z.at[p, n, NZ - k], line_z[k])
 
     def spread(buf, p, plan, use, rest):
@@ -142,7 +142,7 @@
         total = (gram_acc[...] + add).reshape(NY, STRIP, GROUP)
         gram32[g] = total
         gram_part[g] = total.astype(jnp.bfloat16)
-        for k in range(1, NY):
+        for k in (4, 3, 5, 2, 6, 1, 7):
             send(gram_part.at[g, step(y, k, NY)], gram_in.at[g, k], s_g.at[g, k], r_g.at[g, k], line_y[k])
 
     def gram_sum(n, g):
@@ -151,7 +151,7 @@
             arrived(gram_in.at[g, k], s_g.at[g, k], r_g.at[g, k])
             total = total + gram_in[g, k].astype(jnp.float32)
         gram[g, y] = total.astype(jnp.bfloat16)
-        for k in range(1, NY):
+        for k in (4, 3, 5, 2, 6, 1, 7):
             send(gram.at[g, y], gram.at[g, y], s_d.at[g, k], r_d.at[g, k], line_y[k])
 
     def times(buf, n, g):

time: 94.1 us -> 93.5 us (level)
  no operation moved by 1% of the time
where the time goes in v3:
time: 93.5 us; the launch traced here: 93.3 us
  Pallas kernels  91.8 us (98%)
  local copies, waits for them, and re-layouts  1.54 us (2%)
    pallas_call x1, Pallas kernels, body(): pl.pallas_call(kernel, out_shape=jax.ShapeDtypeStruct((HALF, NARROW), bf)...  91.8 us

profile of v3, /device:TPU:1, one launch (start us, length us, event | category | flops | bytes accessed | tf_op | source)
XLA Modules:
  0.0 93.3 jit_solution(8432354972692258154)
XLA Ops:
  0.0 0.0 copy-start
  0.0 0.8 copy-done
  0.8 91.8 %shard_map.17 = bf16[128,224]{1,0:T(8,128)(2,1)S(1)} custom-call(bf16[4,7168]{1,0:T(4,128)(2,1)S(1)} %copy-done), custom_call_target="tpu_custom_call" | custom-call | flops 704643072 | bytes 114688 | tf_op jit(solution)/shard_map/pallas_call | solution.py:262
  92.6 0.7 copy.2
Async XLA Ops:
  0.0 0.8 copy-start
